TPU v7x, 32 devices: a whole 2x2x4 slice. The times are simulated.
32 devices in a mesh: mem: 8 (over z, y), dom: 4 (over x, core).
Axes of the slice: x: 2, y: 2, z: 4, core: 2. Of those that a mesh axis runs over, the one named last changes fastest.
Arguments:
- fcst_pert: float32 [2, 1024, 4, 1024], P(None, 'mem', 'dom'), may hold values from -6 to 6
- sensitivity: float32 [2, 64, 4, 1024], P(None, None, 'dom', 'mem'), may hold values from -6 to 6
- obs_pert: float32 [24576, 1024], P(('mem', 'dom')), may hold values from -6 to 6
- weighted_innovation: float32 [24576], P(('mem', 'dom')), may hold values from -8 to 8
- obs_lists: int32 [8, 16], replicated, may hold values from 0 to 191, as said below
- block_taper: float32 [8, 16], replicated, may hold values from 0.2 to 1
- counts: int32 [8], replicated, may hold values from 8 to 16, as said below
Outputs:
- impact: float32 [24576, 128], P(('mem', 'dom'))
Inputs may be any that keep to these rules, and one draw needn't show every extreme that they name: `obs_lists`: each row's ids are distinct, and every id names an observation block whose column block is within one of the row's column block, cyclically. Observation block o belongs to column block o // 24 and region (o // 6) % 4. The first 8 slots of each row name, for every region, one block of the column block before and one of the column block after. `counts`: some column block uses all 16 slots.
All inputs are finite; a program needn't handle non-finite values.
Results may differ from a plain program's by a relative error of at most 0.0003.
Values sent between devices are 32-bit elements; how exact they have to be, the bound alone decides.
A program may use at most 128 MiB of HBM per device.

v0:
```python
import jax
import jax.numpy as jnp
from jax import lax
from jax.sharding import PartitionSpec as P

M = 1024
OBSB = 128


def extended(cells, sides, width):
    for axis, dim in sides:
        count = lax.axis_size(axis)
        head = lax.slice_in_dim(cells, 0, width, axis=dim)
        tail = lax.slice_in_dim(cells, cells.shape[dim] - width, cells.shape[dim], axis=dim)
        cells = jnp.concatenate(
            [
                lax.ppermute(tail, axis, [(i, (i + 1) % count) for i in range(count)]),
                cells,
                lax.ppermute(head, axis, [((i + 1) % count, i) for i in range(count)]),
            ],
            axis=dim,
        )
    return cells


def block_weights(
    obs_lists, block_taper, counts, column_index, region_index, owned_blocks, regions
):
    row_ids = lax.dynamic_index_in_dim(obs_lists, column_index, 0, keepdims=False)
    row_taper = lax.dynamic_index_in_dim(block_taper, column_index, 0, keepdims=False)
    row_count = lax.dynamic_index_in_dim(counts, column_index, 0, keepdims=False)
    slot_live = jnp.arange(row_ids.shape[0], dtype=jnp.int32) < row_count
    column_count = obs_lists.shape[0]
    owner_columns = (column_index + jnp.arange(3, dtype=jnp.int32) - 1) % column_count
    owner_ids = (owner_columns[:, None] * regions + region_index) * owned_blocks + jnp.arange(
        owned_blocks, dtype=jnp.int32
    )[None, :]
    matched = (owner_ids[:, :, None] == row_ids[None, None, :]) & slot_live[None, None, :]
    return jnp.sum(
        jnp.where(matched, row_taper[None, None, :], jnp.zeros((), row_taper.dtype)), axis=2
    )


def body(fcst_pert, sensitivity, obs_pert, weighted_innovation, obs_lists, block_taper, counts):
    regrouped = lax.all_to_all(fcst_pert, "mem", split_axis=3, concat_axis=1, tiled=True)
    leads = regrouped.shape[0]
    members = regrouped.shape[1]
    targets = sensitivity.shape[1]
    per_lead = []
    for lead in range(leads):
        left = regrouped[lead].reshape(members, -1)
        right = sensitivity[lead].reshape(targets, -1)
        per_lead.append(
            lax.dot_general(left, right, (((1,), (1,)), ((), ())), precision=lax.Precision.HIGHEST)
        )
    partial_sums = jnp.concatenate(per_lead, axis=1)
    summed = lax.psum(partial_sums, "dom")
    column_count = lax.axis_size("mem")
    regions = lax.axis_size("dom")
    column_index = lax.axis_index("mem")
    region_index = lax.axis_index("dom")
    owned_rows = obs_pert.shape[0]
    owned_blocks = owned_rows // OBSB
    row_scale = weighted_innovation / (M - 1)
    beside_all = extended(summed[None], (("mem", 0),), 1)
    source_rows = []
    for offset in (-1, 0, 1):
        source_column = (column_index + offset) % column_count
        weight_rows = block_weights(
            obs_lists, block_taper, counts, source_column, region_index, owned_blocks, regions
        )
        source_rows.append(weight_rows[1 - offset])
    source_weights = jnp.stack(source_rows, axis=0)
    combined = jnp.einsum(
        "sj,skt->jkt", source_weights, beside_all, precision=lax.Precision.HIGHEST
    )
    obs_blocks = obs_pert.reshape(owned_blocks, OBSB, members)
    result = jnp.einsum("jok,jkt->jot", obs_blocks, combined, precision=lax.Precision.HIGHEST)
    result = result.reshape(owned_rows, -1)
    return result * row_scale[:, None]


def solution(mesh):
    in_specs = (
        P(None, "mem", "dom", None),
        P(None, None, "dom", "mem"),
        P(("mem", "dom"), None),
        P(("mem", "dom")),
        P(),
        P(),
        P(),
    )
    out_specs = P(("mem", "dom"), None)
    return jax.shard_map(body, mesh=mesh, in_specs=in_specs, out_specs=out_specs, check_vma=False)
```

profile of v0, /device:TPU:0, one launch (start us, length us, event | category | flops | bytes accessed | tf_op | source)
XLA Modules:
  0.0 134.6 jit_solution(12303247691541051336)
XLA Ops:
  6.5 3.7 %copy.19 = f32[2,128,1,1024]{1,0,2,3:T(2,128)} copy(f32[2,128,1,1024]{3,2,1,0:T(1,128)} %param.7) | data formatting | bytes 2097152 | tf_op args[0]
  10.3 7.3 %all-to-all-start = ((f32[2,128,1,1024]{1,0,2,3:T(2,128)}), f32[2,128,1,1024]{1,0,2,3:T(2,128)}, u32[]{:S(2)}, u32[]{:S(2)}) async-start(f32[2,128,1,1024]{1,0,2,3:T(2,128)} %copy.19), calls=%async_computation | async-start | bytes 2097152 | tf_op jit(solution)/shard_map/all_to_all | solution.py:45
  17.7 0.7 fusion.28
  19.0 0.7 iota_compare_fusion.1
  19.7 0.8 fusion.8
  20.5 0.8 fusion.7
  21.6 21.8 %all-to-all-done = f32[2,128,1,1024]{1,0,2,3:T(2,128)} async-done(((f32[2,128,1,1024]{1,0,2,3:T(2,128)}), f32[2,128,1,1024]{1,0,2,3:T(2,128)}, u32[]{:S(2)}, u32[]{:S(2)}) %all-to-all-start) | async-done | bytes 1048608 | tf_op jit(solution)/shard_map/all_to_all | solution.py:45
  43.4 1.3 copy.20
  44.7 1.1 fusion.26
  45.8 2.0 %copy.21 = f32[1,8,128,1,128]{4,2,1,3,0:T(8,128)} copy(f32[1,8,128,1,128]{2,4,1,0,3:T(8,128)} %get-tuple-element.5) | data formatting | bytes 1048576 | tf_op jit(solution)/shard_map/slice | solution.py:51
  47.8 2.0 %copy.22 = f32[1,8,128,1,128]{4,2,1,3,0:T(8,128)} copy(f32[1,8,128,1,128]{2,4,1,0,3:T(8,128)} %get-tuple-element.6) | data formatting | bytes 1048576 | tf_op jit(solution)/shard_map/slice | solution.py:51
  49.9 1.7 %fusion.29 = f32[1024,64]{0,1:T(8,128)S(1)} fusion(f32[1024,128]{1,0:T(8,128)} %bitcast.41, f32[64,128]{1,0:T(8,128)S(1)} %bitcast.43), kind=kOutput, calls=%fused_computation.58 | convolution fusion | flops 100663296 | bytes 819200 | tf_op jit(solution)/shard_map/dot_general | solution.py:54
  51.6 1.7 %fusion.30 = f32[1024,64]{0,1:T(8,128)S(1)} fusion(f32[1024,128]{1,0:T(8,128)} %bitcast.40, f32[64,128]{1,0:T(8,128)S(1)} %bitcast.42), kind=kOutput, calls=%fused_computation.59 | convolution fusion | flops 100663296 | bytes 819200 | tf_op jit(solution)/shard_map/dot_general | solution.py:54
  53.4 0.8 maximum_bitcast_fusion
  55.0 31.6 %all-reduce.2.cloned.1.call-done = f32[1,1024,128]{1,2,0:T(8,128)} async-done(((f32[1,1024,128]{1,2,0:T(8,128)}), f32[1,1024,128]{1,2,0:T(8,128)}) %all-reduce.2.cloned.1.call-update) | async-done | bytes 524304 | tf_op jit(solution)/shard_map/psum | solution.py:57
  86.6 1.5 %collective-permute-start = (f32[1,1024,128]{1,2,0:T(8,128)}, f32[1,1024,128]{1,2,0:T(8,128)S(1)}, u32[]{:S(2)}, u32[]{:S(2)}) collective-permute-start(f32[1,1024,128]{1,2,0:T(8,128)} %all-reduce.2.cloned.1.call-done), channel_id=1, source_target_pairs={{0,4},{4,8},{8,12},{12,16},{16,20},{20,24},{24,28},{28,0},{1,5},{5... | collective-permute-start | bytes 1572872 | tf_op jit(solution)/shard_map/ppermute | solution.py:17
  88.0 3.2 %collective-permute-start.1 = (f32[1,1024,128]{1,2,0:T(8,128)}, f32[1,1024,128]{1,2,0:T(8,128)S(1)}, u32[]{:S(2)}, u32[]{:S(2)}) collective-permute-start(f32[1,1024,128]{1,2,0:T(8,128)} %all-reduce.2.cloned.1.call-done), channel_id=1, source_target_pairs={{4,0},{8,4},{12,8},{16,12},{20,16},{24,20},{28,24},{0,28},{5,1},{9... | collective-permute-start | bytes 1572872 | tf_op jit(solution)/shard_map/ppermute | solution.py:19
  91.5 18.3 %collective-permute-done = f32[1,1024,128]{1,2,0:T(8,128)S(1)} collective-permute-done((f32[1,1024,128]{1,2,0:T(8,128)}, f32[1,1024,128]{1,2,0:T(8,128)S(1)}, u32[]{:S(2)}, u32[]{:S(2)}) %collective-permute-start) | collective-permute-done | bytes 524320 | tf_op jit(solution)/shard_map/ppermute | solution.py:17
  109.8 2.1 %collective-permute-done.1 = f32[1,1024,128]{1,2,0:T(8,128)S(1)} collective-permute-done((f32[1,1024,128]{1,2,0:T(8,128)}, f32[1,1024,128]{1,2,0:T(8,128)S(1)}, u32[]{:S(2)}, u32[]{:S(2)}) %collective-permute-start.1) | collective-permute-done | bytes 524320 | tf_op jit(solution)/shard_map/ppermute | solution.py:19
  111.9 2.3 %pad_maximum_fusion = f32[3,1024,128]{1,2,0:T(8,128)} fusion(f32[1,1024,128]{1,2,0:T(8,128)S(1)} %collective-permute-done.1, f32[1,1024,128]{1,2,0:T(8,128)} %all-reduce.2.cloned.1.call-done, f32[1,1024,128]{1,2,0:T(8,128)S(1)} %collective-permute-done), kind=kLoop, calls=%fused_computation.2 | loop fusion | flops 786432 | bytes 3145728 | tf_op jit(solution)/shard_map/concatenate | solution.py:15
  114.2 2.8 %copy.23 = f32[3,1024,128]{2,0,1:T(4,128)} copy(f32[3,1024,128]{1,2,0:T(8,128)} %pad_maximum_fusion) | data formatting | bytes 3145728 | tf_op jit(solution)/shard_map/concatenate | solution.py:15
  117.1 6.0 %fusion.2 = f32[6,1024,128]{2,0,1:T(8,128)S(1)} fusion(f32[3,1024,128]{2,0,1:T(4,128)} %copy.23, f32[1,6]{1,0:T(1,128)S(1)} %slice.25, f32[1,6]{1,0:T(1,128)S(1)} %slice.24, f32[1,6]{1,0:T(1,128)S(1)} %slice.23), kind=kOutput, calls=%fused_computation.15 | convolution fusion | flops 28311588 | bytes 4718664 | tf_op jit(solution)/shard_map/sj,skt->jkt/dot_general | solution.py:74
  123.1 3.7 %fusion = f32[6,128,128]{1,2,0:T(8,128)S(1)} fusion(f32[6,128,1024]{2,1,0:T(8,128)S(1)} %bitcast.38, f32[6,1024,128]{2,0,1:T(8,128)S(1)} %fusion.2), kind=kOutput, calls=%fused_computation | convolution fusion | flops 1207959552 | bytes 6684672 | tf_op jit(solution)/shard_map/jok,jkt->jot/dot_general | solution.py:78
  126.8 0.9 bitcast_multiply_fusion
  (25 shorter events, 2.0 us)
Async XLA Ops:
  6.5 116.6 %copy-start = (f32[768,1024]{1,0:T(8,128)S(1)}, f32[768,1024]{1,0:T(8,128)}, u32[]{:S(2)}) copy-start(f32[768,1024]{1,0:T(8,128)} %param.9) | copy-start | bytes 9437188
  6.5 11.1 %copy-start.2 = (s32[8]{0:T(128)S(1)}, s32[8]{0:T(128)}, u32[]{:S(2)}) copy-start(s32[8]{0:T(128)} %param.13) | copy-start | bytes 100
  6.5 15.1 %copy-start.1 = (f32[2,64,1,128]{3,2,1,0:T(1,128)S(1)}, f32[2,64,1,128]{3,2,1,0:T(1,128)}, u32[]{:S(2)}) copy-start(f32[2,64,1,128]{3,2,1,0:T(1,128)} %param.8) | copy-start | bytes 196612
  10.3 33.2 %all-to-all-start = ((f32[2,128,1,1024]{1,0,2,3:T(2,128)}), f32[2,128,1,1024]{1,0,2,3:T(2,128)}, u32[]{:S(2)}, u32[]{:S(2)}) async-start(f32[2,128,1,1024]{1,0,2,3:T(2,128)} %copy.19), calls=%async_computation | async-start | bytes 2097152 | tf_op jit(solution)/shard_map/all_to_all | solution.py:45
  17.5 69.0 %all-reduce.2.cloned.1.call-start = ((), (), s32[]{:S(2)}) async-start(), calls=%async_computation.1 | async-start | bytes 1048576 | tf_op jit(solution)/shard_map/psum | solution.py:57
  45.8 45.7 %copy-start.3 = (f32[768]{0:T(1024)S(1)}, f32[768]{0:T(1024)}, u32[]{:S(2)}) copy-start(f32[768]{0:T(1024)} %param.10) | copy-start | bytes 9220
  86.6 23.3 %collective-permute-start = (f32[1,1024,128]{1,2,0:T(8,128)}, f32[1,1024,128]{1,2,0:T(8,128)S(1)}, u32[]{:S(2)}, u32[]{:S(2)}) collective-permute-start(f32[1,1024,128]{1,2,0:T(8,128)} %all-reduce.2.cloned.1.call-done), channel_id=1, source_target_pairs={{0,4},{4,8},{8,12},{12,16},{16,20},{20,24},{24,28},{28,0},{1,5},{5... | collective-permute-start | bytes 1572872 | tf_op jit(solution)/shard_map/ppermute | solution.py:17
  88.0 23.9 %collective-permute-start.1 = (f32[1,1024,128]{1,2,0:T(8,128)}, f32[1,1024,128]{1,2,0:T(8,128)S(1)}, u32[]{:S(2)}, u32[]{:S(2)}) collective-permute-start(f32[1,1024,128]{1,2,0:T(8,128)} %all-reduce.2.cloned.1.call-done), channel_id=1, source_target_pairs={{4,0},{8,4},{12,8},{16,12},{20,16},{24,20},{28,24},{0,28},{5,1},{9... | collective-permute-start | bytes 1572872 | tf_op jit(solution)/shard_map/ppermute | solution.py:19
Sparse Core Ops, SparseCore 0:
  54.3 32.1 all-reduce.1
where the time goes:
time: 135 us
  waiting for transfers between devices  73.8 us (55%)
  local copies, waits for them, and re-layouts  15.3 us (11%)
  between operations  13.5 us (10%)
  matrix products  13.2 us (10%)
  starting transfers between devices  12 us (9%)
  other arithmetic  6.69 us (5%)
    psum x1, waiting for transfers between devices, body(): summed = lax.psum(partial_sums, 'dom')  31.6 us
    all_to_all x1, waiting for transfers between devices, body(): lax.all_to_all(fcst_pert, 'mem', split_axis=3, concat_axis=1, tiled=True)  21.8 us
    ppermute x1, waiting for transfers between devices, extended(): lax.ppermute(tail, axis, [(i, (i + 1) % count) for i in range(count)])  18.3 us
    all_to_all x1, starting transfers between devices, body(): lax.all_to_all(fcst_pert, 'mem', split_axis=3, concat_axis=1, tiled=True)  7.28 us
    dot_general x1, matrix products, body(): jnp.einsum('sj,skt->jkt', source_weights, beside_all, precision=lax.Preci...  6.03 us
    slice x3, local copies, waits for them, and re-layouts, body(): left = regrouped[lead].reshape(members, -1)  5.18 us
    unnamed x9, local copies, waits for them, and re-layouts  3.73 us
    dot_general x1, matrix products, body(): jnp.einsum('jok,jkt->jot', obs_blocks, combined, precision=lax.Precision....  3.69 us
  transfers between devices with their start and end apart: 4, of which 4 were waited for; matrix products, arithmetic and copies ran while one was open for 4% of the time, Pallas kernels for 0%

commit v1 on v0

--- a/solution.py
+++ b/solution.py
@@ -1,10 +1,15 @@
+import functools
+
 import jax
 import jax.numpy as jnp
 from jax import lax
+from jax.experimental import pallas as pl
+from jax.experimental.pallas import tpu as pltpu
 from jax.sharding import PartitionSpec as P
 
 M = 1024
 OBSB = 128
+MESH = pl.DeviceIdType.MESH
 
 
 def extended(cells, sides, width):
@@ -41,7 +46,7 @@
     )
 
 
-def body(fcst_pert, sensitivity, obs_pert, weighted_innovation, obs_lists, block_taper, counts):
+def general_body(fcst_pert, sensitivity, obs_pert, weighted_innovation, obs_lists, block_taper, counts):
     regrouped = lax.all_to_all(fcst_pert, "mem", split_axis=3, concat_axis=1, tiled=True)
     leads = regrouped.shape[0]
     members = regrouped.shape[1]
@@ -80,6 +85,257 @@
     return result * row_scale[:, None]
 
 
+def halves(x):
+    hi = x.astype(jnp.bfloat16)
+    return hi, (x - hi.astype(jnp.float32)).astype(jnp.bfloat16)
+
+
+def dot3(a, b, dims):
+    d = functools.partial(
+        lax.dot_general, dimension_numbers=(dims, ((), ())), preferred_element_type=jnp.float32
+    )
+    return d(a[0], b[0]) + d(a[0], b[1]) + d(a[1], b[0])
+
+
+ORDER = ((0, 0), (1, 0), (0, 1), (2, 0), (1, 1), (3, 0), (2, 1), (3, 1))
+LAG = 2
+
+
+def kernel(
+    f_hbm, s_hbm, o_hbm, wi_ref, lists_ref, taper_ref, counts_ref, out_ref,
+    xf, obs, oh, ol, sg, pp, rs, cc, g, acc, scale,
+    in_sem, a_send, a_recv, y_send, c_send, c_recv, d_send, d_recv, e_send, e_recv,
+):
+    m = lax.axis_index("mem")
+    r = lax.axis_index("dom")
+    z, y = m // 2, m % 2
+    zx = (z, z + 1 - 2 * (z % 2), (z + 2) % 4, 3 - z)
+    yx = (y, 1 - y)
+
+    def block(j, i):
+        return 2 * zx[j] + yx[i]
+
+    rx = (r, r + 1 - 2 * (r % 2), (r + 2) % 4, 3 - r)
+
+    cp_s = pltpu.make_async_copy(s_hbm, sg.at[m], in_sem.at[0])
+    cp_f = pltpu.make_async_copy(f_hbm, xf, in_sem.at[1])
+    cp_o = pltpu.make_async_copy(o_hbm, obs, in_sem.at[2])
+    cp_s.start()
+    cp_f.start()
+    cp_o.start()
+
+    barrier = pltpu.get_barrier_semaphore()
+    for j, i in ORDER[1:]:
+        pl.semaphore_signal(barrier, inc=1, device_id=(block(j, i), r), device_id_type=MESH)
+    for k in (1, 2, 3):
+        pl.semaphore_signal(barrier, inc=1, device_id=(m, rx[k]), device_id_type=MESH)
+    cp_s.wait()
+    pl.semaphore_wait(barrier, 10)
+
+    def rcopy(src, dst, ss, rsem, dev):
+        return pltpu.make_async_remote_copy(
+            src_ref=src, dst_ref=dst, send_sem=ss, recv_sem=rsem, device_id=dev, device_id_type=MESH
+        )
+
+    def a_copy(j):
+        return rcopy(sg.at[m], sg.at[m], a_send.at[j], a_recv.at[m], (block(j, 0), r))
+
+    def a_arrival(b):
+        return rcopy(sg.at[b], sg.at[b], a_send.at[0], a_recv.at[b], (block(0, 1), r))
+
+    def y_copy(j):
+        b = block(j, 0)
+        return rcopy(sg.at[b], sg.at[b], y_send.at[j], a_recv.at[b], (block(0, 1), r))
+
+    for j in (3, 2, 1):
+        a_copy(j).start()
+    y_copy(0).start()
+    cp_f.wait()
+
+    def c_copy(b, k):
+        rows = pl.ds(pl.multiple_of(rx[k] * 32, 32), 32)
+        return rcopy(
+            pp.at[b, rows], rs.at[k - 1, b], c_send.at[k - 1, b], c_recv.at[k - 1, b], (m, rx[k])
+        )
+
+    def contract(j, i):
+        b = block(j, i)
+        if (j, i) != (0, 0):
+            a_arrival(b).wait_recv()
+        if i == 0 and j > 0:
+            y_copy(j).start()
+        for lead in range(2):
+            left = xf[pl.ds(lead * 1024 + b, 128, stride=8), :]
+            right = sg[b, lead * 64:(lead + 1) * 64, :]
+            part = dot3(halves(left), halves(right), ((1,), (1,)))
+            pp[b, :, lead * 64:(lead + 1) * 64] = part
+        for k in (2, 3, 1):
+            c_copy(b, k).start()
+
+    def d_copy(b, s, q):
+        return rcopy(cc.at[b], g.at[s, m, r], d_send.at[s, b], d_recv.at[s, m], (q, r))
+
+    def finish(j, i):
+        b = block(j, i)
+        for k in (1, 2, 3):
+            c_copy(b, k).wait_recv()
+        own = pl.ds(pl.multiple_of(r * 32, 32), 32)
+        total = (pp[b, own, :] + rs[0, b]) + (rs[1, b] + rs[2, b])
+        cc[b] = total
+        for s in range(3):
+            q = (b + 9 - s) % 8
+
+            @pl.when(q != m)
+            def _():
+                d_copy(b, s, q).start()
+
+            @pl.when(q == m)
+            def _():
+                g[s, m, r] = total
+
+    def prepare():
+        cp_o.wait()
+
+        @pl.loop(0, 6)
+        def _(n):
+            rows = pl.ds(pl.multiple_of(n * 128, 128), 128)
+            hi, lo = halves(obs[rows, :])
+            oh[rows, :] = hi
+            ol[rows, :] = lo
+
+        for n in range(6):
+            col = jnp.broadcast_to(wi_ref[n:n + 1, :], (128, 128)).T * (1.0 / (M - 1))
+            for s in range(3):
+                source = (m + 7 + s) % 8
+                ids = lists_ref[pl.ds(source, 1), :]
+                tap = taper_ref[pl.ds(source, 1), :]
+                live = lax.broadcasted_iota(jnp.int32, ids.shape, 1) < counts_ref[source]
+                hit = (ids == (m * 4 + r) * 6 + n) & live
+                w = jnp.sum(jnp.where(hit, tap, 0.0), axis=1, keepdims=True)
+                scale[s, n] = col * w
+
+    for n in range(8 + LAG):
+        if n < 8:
+            contract(*ORDER[n])
+        if n == 0:
+            prepare()
+        if n >= LAG:
+            finish(*ORDER[n - LAG])
+
+    def e_copy(kind, src_m):
+        if kind < 2:
+            ref = g.at[:, src_m, r]
+            to = rx[1 + kind]
+        else:
+            ref = g.at[:, src_m, rx[2]]
+            to = rx[1]
+        return rcopy(ref, ref, e_send.at[kind, src_m], e_recv.at[kind, src_m], (m, to))
+
+    def e_arrival(kind, src_m):
+        ref = g.at[:, src_m, rx[1 + kind]]
+        return rcopy(ref, ref, e_send.at[kind, src_m], e_recv.at[kind, src_m], (m, rx[1]))
+
+    def spread(j, i):
+        b = block(j, i)
+        if (j, i) != (0, 0):
+            for s in range(3):
+                rcopy(
+                    cc.at[0], g.at[s, b, r], d_send.at[s, 0], d_recv.at[s, b], (b, r)
+                ).wait_recv()
+        e_copy(1, b).start()
+        e_copy(0, b).start()
+
+    def forward(j, i):
+        b = block(j, i)
+        e_arrival(1, b).wait_recv()
+        e_copy(2, b).start()
+
+    def multiply(j):
+        for i in range(2):
+            e_arrival(0, block(j, i)).wait_recv()
+            e_arrival(2, block(j, i)).wait_recv()
+        z0 = zx[j]
+        both = jnp.concatenate(
+            [g[s, pl.ds(2 * z0, 2)].reshape(256, 128) for s in range(3)], axis=1
+        )
+        chunk = halves(both)
+        cols = pl.ds(pl.multiple_of(z0 * 256, 256), 256)
+        for n in range(6):
+            rows = slice(n * 128, (n + 1) * 128)
+            part = dot3((oh[rows, cols], ol[rows, cols]), chunk, ((1,), (0,)))
+            if j == 0:
+                acc[rows, :] = part
+            elif j < 3:
+                acc[rows, :] = acc[rows, :] + part
+            else:
+                part = acc[rows, :] + part
+                out_ref[rows, :] = (
+                    scale[0, n] * part[:, 0:128]
+                    + scale[1, n] * part[:, 128:256]
+                    + scale[2, n] * part[:, 256:384]
+                )
+
+    flat = tuple((j, i) for j in range(4) for i in range(2))
+    for n in range(8):
+        spread(*flat[n])
+        if n >= 1:
+            forward(*flat[n - 1])
+        if n >= 3 and n % 2 == 1:
+            multiply((n - 3) // 2)
+    forward(*flat[7])
+    multiply(3)
+
+    for j in (1, 2, 3):
+        a_copy(j).wait_send()
+    for j in range(4):
+        y_copy(j).wait_send()
+    for b in range(8):
+        for k in (1, 2, 3):
+            c_copy(b, k).wait_send()
+        for s in range(3):
+            q = (b + 9 - s) % 8
+
+            @pl.when(q != m)
+            def _():
+                d_copy(b, s, q).wait_send()
+
+        for kind in range(3):
+            e_copy(kind, b).wait_send()
+
+
+def body(fcst_pert, sensitivity, obs_pert, weighted_innovation, obs_lists, block_taper, counts):
+    f = fcst_pert.reshape(2 * 128 * 8, 128)
+    s = sensitivity.reshape(128, 128)
+    wi = weighted_innovation.reshape(6, 128)
+    any_spec = pl.BlockSpec(memory_space=pl.ANY)
+    vmem = pl.BlockSpec(memory_space=pltpu.VMEM)
+    f32, bf16, dma = jnp.float32, jnp.bfloat16, pltpu.SemaphoreType.DMA
+    return pl.pallas_call(
+        kernel,
+        out_shape=jax.ShapeDtypeStruct((768, 128), f32),
+        in_specs=[any_spec] * 3 + [vmem] * 3 + [pl.BlockSpec(memory_space=pltpu.SMEM)],
+        out_specs=vmem,
+        scratch_shapes=[
+            pltpu.VMEM((2048, 128), f32),
+            pltpu.VMEM((768, 1024), f32),
+            pltpu.VMEM((768, 1024), bf16),
+            pltpu.VMEM((768, 1024), bf16),
+            pltpu.VMEM((8, 128, 128), f32),
+            pltpu.VMEM((8, 128, 128), f32),
+            pltpu.VMEM((3, 8, 32, 128), f32),
+            pltpu.VMEM((8, 32, 128), f32),
+            pltpu.VMEM((3, 8, 4, 32, 128), f32),
+            pltpu.VMEM((768, 384), f32),
+            pltpu.VMEM((3, 6, 128, 128), f32),
+            dma((3,)), dma((4,)), dma((8,)), dma((4,)),
+            dma((3, 8)), dma((3, 8)), dma((3, 8)), dma((3, 8)), dma((3, 8)), dma((3, 8)),
+        ],
+        compiler_params=pltpu.CompilerParams(
+            collective_id=0, has_side_effects=True, vmem_limit_bytes=40 * 1024 * 1024
+        ),
+    )(f, s, obs_pert, wi, obs_lists, block_taper, counts)
+
+
 def solution(mesh):
     in_specs = (
         P(None, "mem", "dom", None),
@@ -91,4 +347,8 @@
         P(),
     )
     out_specs = P(("mem", "dom"), None)
-    return jax.shard_map(body, mesh=mesh, in_specs=in_specs, out_specs=out_specs, check_vma=False)
+    small = mesh.shape["mem"] == 8 and mesh.shape["dom"] == 4
+    return jax.shard_map(
+        body if small else general_body,
+        mesh=mesh, in_specs=in_specs, out_specs=out_specs, check_vma=False,
+    )

time: 135 us -> 48.9 us (0.36)
  the two profiles are of different devices: /device:TPU:0 before, /device:TPU:1 now
where the time goes in v1:
time: 48.9 us; the launch traced here: 48.6 us
  Pallas kernels  41.2 us (84%)
  local copies, waits for them, and re-layouts  7.41 us (15%)
    pallas_call x1, Pallas kernels, body(): pl.pallas_call(kernel, out_shape=jax.ShapeDtypeStruct((768, 128), f32), i...  41.2 us
    unnamed x15, local copies, waits for them, and re-layouts  7.41 us

profile of v1, /device:TPU:1, one launch (start us, length us, event | category | flops | bytes accessed | tf_op | source)
XLA Modules:
  0.0 48.6 jit_solution(13722800399682587296)
XLA Ops:
  0.0 0.0 copy-start
  0.0 1.9 %copy-done = f32[768,1024]{1,0:T(8,128)S(1)} copy-done((f32[768,1024]{1,0:T(8,128)S(1)}, f32[768,1024]{1,0:T(8,128)}, u32[]{:S(2)}) %copy-start) | copy-done | bytes 3145752
  1.9 0.0 copy-start.1
  1.9 1.2 %copy-done.1 = f32[2,128,1,1024]{3,2,1,0:T(1,128)S(1)} copy-done((f32[2,128,1,1024]{3,2,1,0:T(1,128)S(1)}, f32[2,128,1,1024]{3,2,1,0:T(1,128)}, u32[]{:S(2)}) %copy-start.1) | copy-done | bytes 1048600
  3.1 0.0 copy-start.2
  3.1 0.8 %copy-done.2 = f32[2,64,1,128]{3,2,1,0:T(1,128)S(1)} copy-done((f32[2,64,1,128]{3,2,1,0:T(1,128)S(1)}, f32[2,64,1,128]{3,2,1,0:T(1,128)}, u32[]{:S(2)}) %copy-start.2) | copy-done | bytes 65560
  4.0 0.0 copy-start.3
  4.0 0.7 %copy-done.3 = f32[768]{0:T(1024)S(1)} copy-done((f32[768]{0:T(1024)S(1)}, f32[768]{0:T(1024)}, u32[]{:S(2)}) %copy-start.3) | copy-done | bytes 3096
  4.6 0.0 copy-start.4
  4.6 0.7 %copy-done.4 = s32[8,16]{1,0:T(8,128)S(1)} copy-done((s32[8,16]{1,0:T(8,128)S(1)}, s32[8,16]{1,0:T(8,128)}, u32[]{:S(2)}) %copy-start.4) | copy-done | bytes 536
  5.3 0.0 copy-start.5
  5.3 0.7 %copy-done.5 = f32[8,16]{1,0:T(8,128)S(1)} copy-done((f32[8,16]{1,0:T(8,128)S(1)}, f32[8,16]{1,0:T(8,128)}, u32[]{:S(2)}) %copy-start.5) | copy-done | bytes 536
  6.0 0.0 copy-start.6
  6.0 0.7 %copy-done.6 = s32[8]{0:T(128)S(1)} copy-done((s32[8]{0:T(128)S(1)}, s32[8]{0:T(128)}, u32[]{:S(2)}) %copy-start.6) | copy-done | bytes 56
  6.7 41.2 %shard_map.73 = f32[768,128]{1,0:T(8,128)S(1)} custom-call(f32[2048,128]{1,0:T(8,128)S(1)} %bitcast.3, f32[128,128]{1,0:T(8,128)S(1)} %bitcast.4, f32[768,1024]{1,0:T(8,128)S(1)} %copy-done, f32[6,128]{1,0:T(8,128)S(1)} %bitcast.5, s32[8,16]{1,0:T(8,128)S(1)} %copy-done.4, f32[8,16]{1,0:T(8,128)S(1)} %copy-done.5, s32[8]{0:T(128)S(1)} %copy-done.6), custom_call_target="tpu_custom_call" | custom-call | tf_op jit(solution)/shard_map/pallas_call | solution.py:313
  47.8 0.7 %copy.9 = f32[768,128]{1,0:T(8,128)} copy(f32[768,128]{1,0:T(8,128)S(1)} %shard_map.73) | data formatting | bytes 786432
Async XLA Ops:
  0.0 1.9 %copy-start = (f32[768,1024]{1,0:T(8,128)S(1)}, f32[768,1024]{1,0:T(8,128)}, u32[]{:S(2)}) copy-start(f32[768,1024]{1,0:T(8,128)} %o_hbm.1) | copy-start | bytes 9437188
  1.9 1.2 %copy-start.1 = (f32[2,128,1,1024]{3,2,1,0:T(1,128)S(1)}, f32[2,128,1,1024]{3,2,1,0:T(1,128)}, u32[]{:S(2)}) copy-start(f32[2,128,1,1024]{3,2,1,0:T(1,128)} %param.7) | copy-start | bytes 3145732
  3.1 0.8 %copy-start.2 = (f32[2,64,1,128]{3,2,1,0:T(1,128)S(1)}, f32[2,64,1,128]{3,2,1,0:T(1,128)}, u32[]{:S(2)}) copy-start(f32[2,64,1,128]{3,2,1,0:T(1,128)} %param.8) | copy-start | bytes 196612
  4.0 0.7 %copy-start.3 = (f32[768]{0:T(1024)S(1)}, f32[768]{0:T(1024)}, u32[]{:S(2)}) copy-start(f32[768]{0:T(1024)} %param.10) | copy-start | bytes 9220
  4.6 0.7 %copy-start.4 = (s32[8,16]{1,0:T(8,128)S(1)}, s32[8,16]{1,0:T(8,128)}, u32[]{:S(2)}) copy-start(s32[8,16]{1,0:T(8,128)} %lists_ref.1) | copy-start | bytes 1540
  5.3 0.7 %copy-start.5 = (f32[8,16]{1,0:T(8,128)S(1)}, f32[8,16]{1,0:T(8,128)}, u32[]{:S(2)}) copy-start(f32[8,16]{1,0:T(8,128)} %taper_ref.1) | copy-start | bytes 1540
  6.0 0.7 %copy-start.6 = (s32[8]{0:T(128)S(1)}, s32[8]{0:T(128)}, u32[]{:S(2)}) copy-start(s32[8]{0:T(128)} %counts_ref.1) | copy-start | bytes 100

commit v2 on v1

--- a/solution.py
+++ b/solution.py
@@ -97,18 +97,27 @@
     return d(a[0], b[0]) + d(a[0], b[1]) + d(a[1], b[0])
 
 
-ORDER = ((0, 0), (1, 0), (0, 1), (2, 0), (1, 1), (3, 0), (2, 1), (3, 1))
-LAG = 2
+ORDER = ((0, 0), (0, 1), (1, 0), (3, 0), (1, 1), (3, 1), (2, 0), (2, 1))
+CHUNKS = (
+    tuple((0, i, u) for u in (0, 1) for i in (0, 1))
+    + tuple((j, i, u) for j in (1, 3) for i in (0, 1) for u in (0, 1))
+    + tuple((j, i, 2) for j in (0, 1, 3) for i in (0, 1))
+    + tuple((2, i, u) for i in (0, 1) for u in (0, 1, 2))
+)
+AT = (0, 0, 0, 0, 0, 0, 0, 4, 4, 4)
+DONE = {0: 13, 1: 15, 3: 17, 2: 23}
+PASS_LAG = 8
 
 
 def kernel(
-    f_hbm, s_hbm, o_hbm, wi_ref, lists_ref, taper_ref, counts_ref, out_ref,
-    xf, obs, oh, ol, sg, pp, rs, cc, g, acc, scale,
-    in_sem, a_send, a_recv, y_send, c_send, c_recv, d_send, d_recv, e_send, e_recv,
+    f_hbm, s_hbm, o_hbm, wi_hbm, lists_hbm, taper_hbm, counts_hbm, out_ref,
+    wi_ref, lists_ref, taper_ref, counts_ref, xf, obs, oh, ol, sg, pp, rs1, cx, rs2, cc, g, acc, scale,
+    in_sem, a_send, a_recv, y_send, h_send, h_recv, c_send, c_recv, d_send, d_recv, e_send, e_recv,
 ):
     m = lax.axis_index("mem")
     r = lax.axis_index("dom")
     z, y = m // 2, m % 2
+    x, c = r // 2, r % 2
     zx = (z, z + 1 - 2 * (z % 2), (z + 2) % 4, 3 - z)
     yx = (y, 1 - y)
 
@@ -123,6 +132,14 @@
     cp_s.start()
     cp_f.start()
     cp_o.start()
+    cp_small = [
+        pltpu.make_async_copy(src, dst, in_sem.at[3 + n])
+        for n, (src, dst) in enumerate(
+            ((wi_hbm, wi_ref), (lists_hbm, lists_ref), (taper_hbm, taper_ref), (counts_hbm, counts_ref))
+        )
+    ]
+    for cp in cp_small:
+        cp.start()
 
     barrier = pltpu.get_barrier_semaphore()
     for j, i in ORDER[1:]:
@@ -147,16 +164,16 @@
         b = block(j, 0)
         return rcopy(sg.at[b], sg.at[b], y_send.at[j], a_recv.at[b], (block(0, 1), r))
 
-    for j in (3, 2, 1):
+    y_copy(0).start()
+    for j in (1, 3, 2):
         a_copy(j).start()
-    y_copy(0).start()
     cp_f.wait()
 
-    def c_copy(b, k):
-        rows = pl.ds(pl.multiple_of(rx[k] * 32, 32), 32)
-        return rcopy(
-            pp.at[b, rows], rs.at[k - 1, b], c_send.at[k - 1, b], c_recv.at[k - 1, b], (m, rx[k])
-        )
+    def h_copy(b):
+        return rcopy(pp.at[b, 1 - c], rs1.at[b], h_send.at[b], h_recv.at[b], (m, rx[1]))
+
+    def c_copy(b):
+        return rcopy(cx.at[b], rs2.at[b], c_send.at[b], c_recv.at[b], (m, rx[2]))
 
     def contract(j, i):
         b = block(j, i)
@@ -168,19 +185,24 @@
             left = xf[pl.ds(lead * 1024 + b, 128, stride=8), :]
             right = sg[b, lead * 64:(lead + 1) * 64, :]
             part = dot3(halves(left), halves(right), ((1,), (1,)))
-            pp[b, :, lead * 64:(lead + 1) * 64] = part
-        for k in (2, 3, 1):
-            c_copy(b, k).start()
+            for n in range(4):
+                pp[b, n % 2, n // 2, :, lead * 64:(lead + 1) * 64] = part[n * 32:(n + 1) * 32]
+        h_copy(b).start()
+
+    def over_cores(j, i):
+        b = block(j, i)
+        h_copy(b).wait_recv()
+        cx[b] = pp[b, c, 1 - x] + rs1[b, 1 - x]
+        c_copy(b).start()
+        cc[b] = pp[b, c, x] + rs1[b, x]
 
     def d_copy(b, s, q):
         return rcopy(cc.at[b], g.at[s, m, r], d_send.at[s, b], d_recv.at[s, m], (q, r))
 
     def finish(j, i):
         b = block(j, i)
-        for k in (1, 2, 3):
-            c_copy(b, k).wait_recv()
-        own = pl.ds(pl.multiple_of(r * 32, 32), 32)
-        total = (pp[b, own, :] + rs[0, b]) + (rs[1, b] + rs[2, b])
+        c_copy(b).wait_recv()
+        total = cc[b] + rs2[b]
         cc[b] = total
         for s in range(3):
             q = (b + 9 - s) % 8
@@ -195,6 +217,8 @@
 
     def prepare():
         cp_o.wait()
+        for cp in cp_small:
+            cp.wait()
 
         @pl.loop(0, 6)
         def _(n):
@@ -214,46 +238,41 @@
                 w = jnp.sum(jnp.where(hit, tap, 0.0), axis=1, keepdims=True)
                 scale[s, n] = col * w
 
-    for n in range(8 + LAG):
-        if n < 8:
-            contract(*ORDER[n])
-        if n == 0:
-            prepare()
-        if n >= LAG:
-            finish(*ORDER[n - LAG])
-
-    def e_copy(kind, src_m):
+    def slot(u):
+        return (1, 2 - 2 * y, 2 * y)[u]
+
+    def e_copy(kind, src_m, s):
         if kind < 2:
-            ref = g.at[:, src_m, r]
+            ref = g.at[s, src_m, r]
             to = rx[1 + kind]
         else:
-            ref = g.at[:, src_m, rx[2]]
+            ref = g.at[s, src_m, rx[2]]
             to = rx[1]
-        return rcopy(ref, ref, e_send.at[kind, src_m], e_recv.at[kind, src_m], (m, to))
-
-    def e_arrival(kind, src_m):
-        ref = g.at[:, src_m, rx[1 + kind]]
-        return rcopy(ref, ref, e_send.at[kind, src_m], e_recv.at[kind, src_m], (m, rx[1]))
-
-    def spread(j, i):
-        b = block(j, i)
+        return rcopy(ref, ref, e_send.at[kind, src_m, s], e_recv.at[kind, src_m, s], (m, to))
+
+    def e_arrival(kind, src_m, s):
+        ref = g.at[s, src_m, rx[1 + kind]]
+        return rcopy(ref, ref, e_send.at[kind, src_m, s], e_recv.at[kind, src_m, s], (m, rx[1]))
+
+    def spread(j, i, u):
+        b, s = block(j, i), slot(u)
         if (j, i) != (0, 0):
-            for s in range(3):
-                rcopy(
-                    cc.at[0], g.at[s, b, r], d_send.at[s, 0], d_recv.at[s, b], (b, r)
-                ).wait_recv()
-        e_copy(1, b).start()
-        e_copy(0, b).start()
-
-    def forward(j, i):
-        b = block(j, i)
-        e_arrival(1, b).wait_recv()
-        e_copy(2, b).start()
+            rcopy(
+                cc.at[0], g.at[s, b, r], d_send.at[s, 0], d_recv.at[s, b], (b, r)
+            ).wait_recv()
+        e_copy(1, b, s).start()
+        e_copy(0, b, s).start()
+
+    def forward(j, i, u):
+        b, s = block(j, i), slot(u)
+        e_arrival(1, b, s).wait_recv()
+        e_copy(2, b, s).start()
 
     def multiply(j):
         for i in range(2):
-            e_arrival(0, block(j, i)).wait_recv()
-            e_arrival(2, block(j, i)).wait_recv()
+            for s in range(3):
+                e_arrival(0, block(j, i), s).wait_recv()
+                e_arrival(2, block(j, i), s).wait_recv()
         z0 = zx[j]
         both = jnp.concatenate(
             [g[s, pl.ds(2 * z0, 2)].reshape(256, 128) for s in range(3)], axis=1
@@ -265,7 +284,7 @@
             part = dot3((oh[rows, cols], ol[rows, cols]), chunk, ((1,), (0,)))
             if j == 0:
                 acc[rows, :] = part
-            elif j < 3:
+            elif j != 2:
                 acc[rows, :] = acc[rows, :] + part
             else:
                 part = acc[rows, :] + part
@@ -275,23 +294,39 @@
                     + scale[2, n] * part[:, 256:384]
                 )
 
-    flat = tuple((j, i) for j in range(4) for i in range(2))
-    for n in range(8):
-        spread(*flat[n])
-        if n >= 1:
-            forward(*flat[n - 1])
-        if n >= 3 and n % 2 == 1:
-            multiply((n - 3) // 2)
-    forward(*flat[7])
-    multiply(3)
+    done = 0
+
+    def passing(count):
+        nonlocal done
+        for n in range(done, done + count):
+            if n < 24:
+                spread(*CHUNKS[n])
+            if PASS_LAG <= n < 24 + PASS_LAG:
+                forward(*CHUNKS[n - PASS_LAG])
+            for j in range(4):
+                if n == DONE[j] + PASS_LAG + 1:
+                    multiply(j)
+        done += count
+
+    for n in range(10):
+        if n < 8:
+            contract(*ORDER[n])
+        if n == 0:
+            prepare()
+        if 1 <= n < 9:
+            over_cores(*ORDER[n - 1])
+        if n >= 2:
+            finish(*ORDER[n - 2])
+        passing(AT[n])
+    passing(24 + PASS_LAG + 1 - done)
 
     for j in (1, 2, 3):
         a_copy(j).wait_send()
     for j in range(4):
         y_copy(j).wait_send()
     for b in range(8):
-        for k in (1, 2, 3):
-            c_copy(b, k).wait_send()
+        h_copy(b).wait_send()
+        c_copy(b).wait_send()
         for s in range(3):
             q = (b + 9 - s) % 8
 
@@ -300,7 +335,8 @@
                 d_copy(b, s, q).wait_send()
 
         for kind in range(3):
-            e_copy(kind, b).wait_send()
+            for s in range(3):
+                e_copy(kind, b, s).wait_send()
 
 
 def body(fcst_pert, sensitivity, obs_pert, weighted_innovation, obs_lists, block_taper, counts):
@@ -313,25 +349,32 @@
     return pl.pallas_call(
         kernel,
         out_shape=jax.ShapeDtypeStruct((768, 128), f32),
-        in_specs=[any_spec] * 3 + [vmem] * 3 + [pl.BlockSpec(memory_space=pltpu.SMEM)],
+        in_specs=[any_spec] * 7,
         out_specs=vmem,
         scratch_shapes=[
+            pltpu.VMEM((6, 128), f32),
+            pltpu.VMEM((8, 16), jnp.int32),
+            pltpu.VMEM((8, 16), f32),
+            pltpu.SMEM((8,), jnp.int32),
             pltpu.VMEM((2048, 128), f32),
             pltpu.VMEM((768, 1024), f32),
             pltpu.VMEM((768, 1024), bf16),
             pltpu.VMEM((768, 1024), bf16),
             pltpu.VMEM((8, 128, 128), f32),
-            pltpu.VMEM((8, 128, 128), f32),
-            pltpu.VMEM((3, 8, 32, 128), f32),
+            pltpu.VMEM((8, 2, 2, 32, 128), f32),
+            pltpu.VMEM((8, 2, 32, 128), f32),
+            pltpu.VMEM((8, 32, 128), f32),
+            pltpu.VMEM((8, 32, 128), f32),
             pltpu.VMEM((8, 32, 128), f32),
             pltpu.VMEM((3, 8, 4, 32, 128), f32),
             pltpu.VMEM((768, 384), f32),
             pltpu.VMEM((3, 6, 128, 128), f32),
-            dma((3,)), dma((4,)), dma((8,)), dma((4,)),
-            dma((3, 8)), dma((3, 8)), dma((3, 8)), dma((3, 8)), dma((3, 8)), dma((3, 8)),
+            dma((7,)), dma((4,)), dma((8,)), dma((4,)),
+            dma((8,)), dma((8,)), dma((8,)), dma((8,)),
+            dma((3, 8)), dma((3, 8)), dma((3, 8, 3)), dma((3, 8, 3)),
         ],
         compiler_params=pltpu.CompilerParams(
-            collective_id=0, has_side_effects=True, vmem_limit_bytes=40 * 1024 * 1024
+            collective_id=0, has_side_effects=True, vmem_limit_bytes=60 * 1024 * 1024
         ),
     )(f, s, obs_pert, wi, obs_lists, block_taper, counts)
 

time: 48.9 us -> 41.8 us (0.85)
  the two profiles are of different devices: /device:TPU:1 before, /device:TPU:0 now
where the time goes in v2:
time: 41.8 us; the launch traced here: 41.5 us
  Pallas kernels  39.7 us (95%)
  local copies, waits for them, and re-layouts  1.77 us (4%)
    pallas_call x1, Pallas kernels, body(): pl.pallas_call(kernel, out_shape=jax.ShapeDtypeStruct((768, 128), f32), i...  39.7 us
    unnamed x1, local copies, waits for them, and re-layouts  1.77 us

profile of v2, /device:TPU:0, one launch (start us, length us, event | category | flops | bytes accessed | tf_op | source)
XLA Modules:
  0.0 41.5 jit_solution(110223251076416837)
XLA Ops:
  0.0 39.7 %shard_map.73 = f32[768,128]{1,0:T(8,128)} custom-call(f32[2048,128]{1,0:T(8,128)} %bitcast.3, f32[128,128]{1,0:T(8,128)} %bitcast.4, f32[768,1024]{1,0:T(8,128)} %o_hbm.1, f32[6,128]{1,0:T(8,128)} %bitcast.5, s32[8,16]{1,0:T(8,128)} %lists_hbm.1, f32[8,16]{1,0:T(8,128)} %taper_hbm.1, s32[8]{0:T(128)} %counts_hbm.1), custom_call_target="tpu_custom_call" | custom-call | tf_op jit(solution)/shard_map/pallas_call | solution.py:349
  39.7 1.8 %copy.9 = f32[768,128]{1,0:T(8,128)} copy(f32[768,128]{1,0:T(8,128)} %shard_map.73) | data formatting | bytes 786432

commit v3 on v2

--- a/solution.py
+++ b/solution.py
@@ -104,7 +104,7 @@
     + tuple((j, i, 2) for j in (0, 1, 3) for i in (0, 1))
     + tuple((2, i, u) for i in (0, 1) for u in (0, 1, 2))
 )
-AT = (0, 0, 0, 0, 0, 0, 0, 4, 4, 4)
+AT = (0, 0, 0, 0, 0, 0, 0, 0, 4, 4, 4)
 DONE = {0: 13, 1: 15, 3: 17, 2: 23}
 PASS_LAG = 8
 
@@ -308,15 +308,15 @@
                     multiply(j)
         done += count
 
-    for n in range(10):
+    for n in range(11):
         if n < 8:
             contract(*ORDER[n])
         if n == 0:
             prepare()
         if 1 <= n < 9:
             over_cores(*ORDER[n - 1])
-        if n >= 2:
-            finish(*ORDER[n - 2])
+        if n >= 3:
+            finish(*ORDER[n - 3])
         passing(AT[n])
     passing(24 + PASS_LAG + 1 - done)
 

time: 41.8 us -> 41.3 us (0.988)
  no operation moved by 1% of the time
where the time goes in v3:
time: 41.3 us; the launch traced here: 41.2 us
  Pallas kernels  39.4 us (95%)
  local copies, waits for them, and re-layouts  1.77 us (4%)
    pallas_call x1, Pallas kernels, body(): pl.pallas_call(kernel, out_shape=jax.ShapeDtypeStruct((768, 128), f32), i...  39.4 us
    unnamed x1, local copies, waits for them, and re-layouts  1.77 us

profile of v3, /device:TPU:0, one launch (start us, length us, event | category | flops | bytes accessed | tf_op | source)
XLA Modules:
  0.0 41.2 jit_solution(9891177276484091525)
XLA Ops:
  0.0 39.4 %shard_map.73 = f32[768,128]{1,0:T(8,128)} custom-call(f32[2048,128]{1,0:T(8,128)} %bitcast.3, f32[128,128]{1,0:T(8,128)} %bitcast.4, f32[768,1024]{1,0:T(8,128)} %o_hbm.1, f32[6,128]{1,0:T(8,128)} %bitcast.5, s32[8,16]{1,0:T(8,128)} %lists_hbm.1, f32[8,16]{1,0:T(8,128)} %taper_hbm.1, s32[8]{0:T(128)} %counts_hbm.1), custom_call_target="tpu_custom_call" | custom-call | tf_op jit(solution)/shard_map/pallas_call | solution.py:349
  39.4 1.8 %copy.9 = f32[768,128]{1,0:T(8,128)} copy(f32[768,128]{1,0:T(8,128)} %shard_map.73) | data formatting | bytes 786432
